TPU v7x, 32 devices: a whole 2x2x4 slice. The times are simulated.
32 devices in a mesh: sx: 8 (over z, y), sy: 4 (over x, core).
Axes of the slice: x: 2, y: 2, z: 4, core: 2. Of those that a mesh axis runs over, the one named last changes fastest.
Arguments:
- dual_ops: bfloat16 [8, 4, 2048, 2048], P('sx', 'sy'), may hold values from -0.028726213 to 1.0287262
- loads: float32 [8, 4, 2048, 128], P('sx', 'sy'), may hold values from -6 to 6
- kernel_basis: bfloat16 [8, 4, 64, 2048], P('sx', 'sy'), may hold values from -0.13183594 to 0.13183594
- coarse_inverse: bfloat16 [8, 4, 256, 512], P('sx', 'sy'), may hold values from -1 to 1
Outputs:
- multipliers: float32 [8, 4, 2048, 128], P('sx', 'sy')
All inputs are finite; a program needn't handle non-finite values.
Results may differ from a plain program's by a relative error of at most 0.0085.
Values may be sent and summed in bfloat16 or wider, within the bound.
A program may use at most 64 MiB of HBM per device.

v0:
```python
import jax
import jax.numpy as jnp
from jax import lax
from jax.sharding import PartitionSpec as P

ITERS = 3


damping = 0.5


def with_halo(block, sides, width):
    for axis, dim in sides:
        count = lax.axis_size(axis)
        forward = [(i, i + 1) for i in range(count - 1)]
        backward = [(target, source) for source, target in forward]
        low = lax.ppermute(
            lax.slice_in_dim(block, block.shape[dim] - width, None, axis=dim), axis, forward
        )
        high = lax.ppermute(lax.slice_in_dim(block, 0, width, axis=dim), axis, backward)
        block = jnp.concatenate([low, block, high], axis=dim)
    return block


def combine_faces(values, vertical, beside):
    width = values.shape[0] // 4
    return jnp.concatenate(
        [
            values[:width] - vertical[0],
            values[width : 2 * width] - vertical[3],
            values[2 * width : 3 * width] - beside[0],
            values[3 * width :] - beside[3],
        ],
        axis=0,
    )


def residual_faces(values):
    width = values.shape[0] // 4
    vertical = with_halo(jnp.stack([values[:width], values[width : 2 * width]]), (("sx", 0),), 1)
    beside = with_halo(
        jnp.stack([values[2 * width : 3 * width], values[3 * width :]]), (("sy", 0),), 1
    )
    return combine_faces(values, vertical, beside)


def correction_faces(values):
    width = values.shape[0] // 4
    vertical = with_halo(
        jnp.stack([values[:width], values[width : 2 * width]]).astype(jnp.bfloat16), (("sx", 0),), 1
    ).astype(jnp.float32)
    beside = with_halo(
        jnp.stack([values[2 * width : 3 * width], values[3 * width :]]).astype(jnp.bfloat16),
        (("sy", 0),),
        1,
    ).astype(jnp.float32)
    return combine_faces(values, vertical, beside)


def spread_back(columns, weights):
    return lax.dot_general(
        columns, weights, (((0,), (0,)), ((), ())), preferred_element_type=jnp.float32
    )


def local(dual_ops, loads, kernel_basis, coarse_inverse):
    operator = dual_ops[0, 0]
    right_side = loads[0, 0]
    basis = kernel_basis[0, 0]
    tile = coarse_inverse[0, 0]
    multipliers = jnp.zeros(right_side.shape, jnp.float32)
    for step in range(ITERS):
        product = jnp.dot(
            operator, multipliers.astype(jnp.bfloat16), preferred_element_type=jnp.float32
        )
        residual = residual_faces(right_side - product)
        coarse_in = jnp.dot(
            basis, residual.astype(jnp.bfloat16), preferred_element_type=jnp.float32
        ).astype(jnp.bfloat16)
        partial_rows = jnp.dot(
            tile,
            lax.all_gather(coarse_in, "sx", axis=0, tiled=True),
            preferred_element_type=jnp.float32,
        )
        coarse_out = lax.psum_scatter(partial_rows, "sy", scatter_dimension=0, tiled=True).astype(
            jnp.bfloat16
        )
        back = spread_back(basis, coarse_out)
        correction = correction_faces(back)
        multipliers = multipliers + damping * (residual - correction)
    return multipliers[None, None]


def solution(mesh):
    placed = (
        P("sx", "sy", None, None),
        P("sx", "sy", None, None),
        P("sx", "sy", None, None),
        P("sx", "sy", None, None),
    )
    return jax.shard_map(
        local, mesh=mesh, in_specs=placed, out_specs=P("sx", "sy", None, None), check_vma=False
    )
```

profile of v0, /device:TPU:0, one launch (start us, length us, event | category | flops | bytes accessed | tf_op | source)
XLA Modules:
  0.0 306.5 jit_solution(12758523559578870158)
XLA Ops:
  6.5 1.6 copy.7
  8.2 6.3 %fusion.21 = f32[2048,128]{0,1:T(8,128)S(1)} fusion(bf16[1,1,2048,2048]{3,2,1,0:T(8,128)(2,1)} %param.4, f32[1,1,2048,128]{2,3,1,0:T(8,128)S(1)} %copy.7), kind=kOutput, calls=%fused_computation.14 | convolution fusion | flops 1074003968 | bytes 10485760 | tf_op jit(solution)/shard_map/dot_general | solution.py:73
  14.4 4.9 %collective-permute-start = (f32[1,512,128]{1,2,0:T(8,128)S(1)}, f32[1,512,128]{1,2,0:T(8,128)S(1)}, u32[]{:S(2)}, u32[]{:S(2)}) collective-permute-start(f32[1,512,128]{1,2,0:T(8,128)S(1)} %slice_bitcast_fusion.10), channel_id=1, source_target_pairs={{0,4},{4,8},{8,12},{12,16},{16,20},{20,24},{24,28},{1,5},{5,9},{9,... | collective-permute-start | bytes 786440 | tf_op jit(solution)/shard_map/ppermute | solution.py:17
  19.3 5.5 %collective-permute-done = f32[1,512,128]{1,2,0:T(8,128)S(1)} collective-permute-done((f32[1,512,128]{1,2,0:T(8,128)S(1)}, f32[1,512,128]{1,2,0:T(8,128)S(1)}, u32[]{:S(2)}, u32[]{:S(2)}) %collective-permute-start) | collective-permute-done | bytes 262176 | tf_op jit(solution)/shard_map/ppermute | solution.py:17
  27.6 3.0 collective-permute-start.2
  30.7 4.2 %collective-permute-done.1 = f32[1,512,128]{1,2,0:T(8,128)S(1)} collective-permute-done((f32[1,512,128]{1,2,0:T(8,128)S(1)}, f32[1,512,128]{1,2,0:T(8,128)S(1)}, u32[]{:S(2)}, u32[]{:S(2)}) %collective-permute-start.1) | collective-permute-done | bytes 262176 | tf_op jit(solution)/shard_map/ppermute | solution.py:20
  35.3 32.0 %all_gather.9 = bf16[512,128]{1,0:T(8,128)(2,1)S(1)} all-gather(bf16[64,128]{1,0:T(8,128)(2,1)S(1)} %fusion.24), channel_id=1, replica_groups=mesh['sx'=8,'sy'=4] {'sx'}, dimensions={0}, use_global_device_ids=true | all-gather | bytes 147456 | tf_op jit(solution)/shard_map/all_gather | solution.py:82
  68.3 23.6 %reduce-scatter.10.cloned.1.call-done = f32[64,128]{1,0:T(8,128)} async-done(((f32[256,128]{1,0:T(8,128)}), f32[64,128]{1,0:T(8,128)}) %reduce-scatter.10.cloned.1.call-update) | async-done | bytes 32784
  95.8 3.4 %collective-permute-start.4 = (bf16[1,512,128]{1,2,0:T(8,128)(2,1)S(1)}, bf16[1,512,128]{1,2,0:T(8,128)(2,1)S(1)}, u32[]{:S(2)}, u32[]{:S(2)}) collective-permute-start(bf16[1,512,128]{1,2,0:T(8,128)(2,1)S(1)} %get-tuple-element.50), channel_id=1, source_target_pairs={{0,4},{4,8},{8,12},{12,16},{16,20},{20,24},{24,28},{1,5},{5,9},{9,... | collective-permute-start | bytes 393224 | tf_op jit(solution)/shard_map/ppermute | solution.py:17
  100.5 1.5 collective-permute-done.4
  102.1 4.7 %collective-permute-done.5 = bf16[1,512,128]{1,2,0:T(8,128)(2,1)S(1)} collective-permute-done((bf16[1,512,128]{1,2,0:T(8,128)(2,1)S(1)}, bf16[1,512,128]{1,2,0:T(8,128)(2,1)S(1)}, u32[]{:S(2)}, u32[]{:S(2)}) %collective-permute-start.5) | collective-permute-done | bytes 131104 | tf_op jit(solution)/shard_map/ppermute | solution.py:20
  106.9 6.4 %fusion.18 = f32[2048,128]{0,1:T(8,128)S(1)} fusion(bf16[1,1,2048,2048]{3,2,1,0:T(8,128)(2,1)} %param.4, f32[1,1,2048,128]{2,3,1,0:T(8,128)S(1)} %copy.7, f32[512,128]{0,1:T(8,128)S(1)} %get-tuple-element.16, f32[512,128]{0,1:T(8,128)S(1)} %get-tuple-element.15, f32[512,128]{0,1:T(8,128)S(1)} %get-tuple-element.14, f32[512,128]{0,1:T(8,128)S(1)} %get-tuple-element.13, ...), kind=kOutput, calls=%fused_computation.13 | convolution fusion | flops 1076363264 | bytes 12582912 | tf_op jit(solution)/shard_map/dot_general | solution.py:73
  113.3 4.3 %collective-permute-start.8 = (f32[1,512,128]{1,2,0:T(8,128)S(1)}, f32[1,512,128]{1,2,0:T(8,128)S(1)}, u32[]{:S(2)}, u32[]{:S(2)}) collective-permute-start(f32[1,512,128]{1,2,0:T(8,128)S(1)} %slice_bitcast_fusion.6), channel_id=1, source_target_pairs={{0,4},{4,8},{8,12},{12,16},{16,20},{20,24},{24,28},{1,5},{5,9},{9,... | collective-permute-start | bytes 786440 | tf_op jit(solution)/shard_map/ppermute | solution.py:17
  117.5 6.2 %collective-permute-done.8 = f32[1,512,128]{1,2,0:T(8,128)S(1)} collective-permute-done((f32[1,512,128]{1,2,0:T(8,128)S(1)}, f32[1,512,128]{1,2,0:T(8,128)S(1)}, u32[]{:S(2)}, u32[]{:S(2)}) %collective-permute-start.8) | collective-permute-done | bytes 262176 | tf_op jit(solution)/shard_map/ppermute | solution.py:17
  126.4 3.0 collective-permute-start.10
  129.5 4.9 %collective-permute-done.9 = f32[1,512,128]{1,2,0:T(8,128)S(1)} collective-permute-done((f32[1,512,128]{1,2,0:T(8,128)S(1)}, f32[1,512,128]{1,2,0:T(8,128)S(1)}, u32[]{:S(2)}, u32[]{:S(2)}) %collective-permute-start.9) | collective-permute-done | bytes 262176 | tf_op jit(solution)/shard_map/ppermute | solution.py:20
  135.5 30.9 %all_gather.10 = bf16[512,128]{1,0:T(8,128)(2,1)S(1)} all-gather(bf16[64,128]{1,0:T(8,128)(2,1)S(1)} %fusion.25), channel_id=1, replica_groups=mesh['sx'=8,'sy'=4] {'sx'}, dimensions={0}, use_global_device_ids=true | all-gather | bytes 147456 | tf_op jit(solution)/shard_map/all_gather | solution.py:82
  167.5 22.9 %reduce-scatter.12.cloned.1.call-done = f32[64,128]{1,0:T(8,128)} async-done(((f32[256,128]{1,0:T(8,128)}), f32[64,128]{1,0:T(8,128)}) %reduce-scatter.12.cloned.1.call-update) | async-done | bytes 32784
  194.2 3.4 %collective-permute-start.12 = (bf16[1,512,128]{1,2,0:T(8,128)(2,1)S(1)}, bf16[1,512,128]{1,2,0:T(8,128)(2,1)S(1)}, u32[]{:S(2)}, u32[]{:S(2)}) collective-permute-start(bf16[1,512,128]{1,2,0:T(8,128)(2,1)S(1)} %get-tuple-element.39), channel_id=1, source_target_pairs={{0,4},{4,8},{8,12},{12,16},{16,20},{20,24},{24,28},{1,5},{5,9},{9,... | collective-permute-start | bytes 393224 | tf_op jit(solution)/shard_map/ppermute | solution.py:17
  199.0 1.5 collective-permute-done.12
  200.6 4.7 %collective-permute-done.13 = bf16[1,512,128]{1,2,0:T(8,128)(2,1)S(1)} collective-permute-done((bf16[1,512,128]{1,2,0:T(8,128)(2,1)S(1)}, bf16[1,512,128]{1,2,0:T(8,128)(2,1)S(1)}, u32[]{:S(2)}, u32[]{:S(2)}) %collective-permute-start.13) | collective-permute-done | bytes 131104 | tf_op jit(solution)/shard_map/ppermute | solution.py:20
  205.4 6.9 %fusion.15 = f32[2048,128]{0,1:T(8,128)S(1)} fusion(bf16[1,1,2048,2048]{3,2,1,0:T(8,128)(2,1)} %param.4, f32[1,1,2048,128]{2,3,1,0:T(8,128)S(1)} %copy.7, f32[512,128]{0,1:T(8,128)S(1)} %get-tuple-element.12, f32[512,128]{0,1:T(8,128)S(1)} %get-tuple-element.11, f32[512,128]{0,1:T(8,128)S(1)} %get-tuple-element.10, f32[512,128]{0,1:T(8,128)S(1)} %get-tuple-element.9, ...), kind=kOutput, calls=%fused_computation.12 | convolution fusion | flops 1078722560 | bytes 14680064 | tf_op jit(solution)/shard_map/dot_general | solution.py:73
  212.4 4.3 %collective-permute-start.16 = (f32[1,512,128]{1,2,0:T(8,128)S(1)}, f32[1,512,128]{1,2,0:T(8,128)S(1)}, u32[]{:S(2)}, u32[]{:S(2)}) collective-permute-start(f32[1,512,128]{1,2,0:T(8,128)S(1)} %get-tuple-element.35), channel_id=1, source_target_pairs={{0,4},{4,8},{8,12},{12,16},{16,20},{20,24},{24,28},{1,5},{5,9},{9,... | collective-permute-start | bytes 786440 | tf_op jit(solution)/shard_map/ppermute | solution.py:17
  219.3 3.0 collective-permute-start.18
  222.3 6.1 %collective-permute-done.16 = f32[1,512,128]{1,2,0:T(8,128)S(1)} collective-permute-done((f32[1,512,128]{1,2,0:T(8,128)S(1)}, f32[1,512,128]{1,2,0:T(8,128)S(1)}, u32[]{:S(2)}, u32[]{:S(2)}) %collective-permute-start.16) | collective-permute-done | bytes 262176 | tf_op jit(solution)/shard_map/ppermute | solution.py:17
  229.9 31.9 %all_gather.11 = bf16[512,128]{1,0:T(8,128)(2,1)S(1)} all-gather(bf16[64,128]{1,0:T(8,128)(2,1)S(1)} %fusion.26), channel_id=1, replica_groups=mesh['sx'=8,'sy'=4] {'sx'}, dimensions={0}, use_global_device_ids=true | all-gather | bytes 147456 | tf_op jit(solution)/shard_map/all_gather | solution.py:82
  262.8 18.8 %reduce-scatter.14.cloned.1.call-done = f32[64,128]{1,0:T(8,128)} async-done(((f32[256,128]{1,0:T(8,128)}), f32[64,128]{1,0:T(8,128)}) %reduce-scatter.14.cloned.1.call-update) | async-done | bytes 32784
  285.4 3.4 %collective-permute-start.20 = (bf16[1,512,128]{1,2,0:T(8,128)(2,1)S(1)}, bf16[1,512,128]{1,2,0:T(8,128)(2,1)S(1)}, u32[]{:S(2)}, u32[]{:S(2)}) collective-permute-start(bf16[1,512,128]{1,2,0:T(8,128)(2,1)S(1)} %get-tuple-element.25), channel_id=1, source_target_pairs={{0,4},{4,8},{8,12},{12,16},{16,20},{20,24},{24,28},{1,5},{5,9},{9,... | collective-permute-start | bytes 393224 | tf_op jit(solution)/shard_map/ppermute | solution.py:17
  290.2 1.5 collective-permute-done.20
  291.8 4.7 %collective-permute-done.21 = bf16[1,512,128]{1,2,0:T(8,128)(2,1)S(1)} collective-permute-done((bf16[1,512,128]{1,2,0:T(8,128)(2,1)S(1)}, bf16[1,512,128]{1,2,0:T(8,128)(2,1)S(1)}, u32[]{:S(2)}, u32[]{:S(2)}) %collective-permute-start.21) | collective-permute-done | bytes 131104 | tf_op jit(solution)/shard_map/ppermute | solution.py:20
  296.5 2.2 fusion.29
  298.7 1.3 copy.8
  (90 shorter events, 29.9 us)
Async XLA Ops:
  6.5 28.4 %copy-start = (bf16[1,1,64,2048]{3,2,1,0:T(8,128)(2,1)S(1)}, bf16[1,1,64,2048]{3,2,1,0:T(8,128)(2,1)}, u32[]{:S(2)}) copy-start(bf16[1,1,64,2048]{3,2,1,0:T(8,128)(2,1)} %param.6) | copy-start | bytes 786436
  6.5 85.4 %reduce-scatter.10.cloned.1.call-start = ((), (), s32[]{:S(2)}) async-start(), calls=%async_computation.3 | async-start | bytes 163840
  8.1 59.1 %copy-start.1 = (bf16[1,1,256,512]{3,2,1,0:T(8,128)(2,1)S(1)}, bf16[1,1,256,512]{3,2,1,0:T(8,128)(2,1)}, u32[]{:S(2)}) copy-start(bf16[1,1,256,512]{3,2,1,0:T(8,128)(2,1)} %param.7) | copy-start | bytes 786436
  14.4 10.4 %collective-permute-start = (f32[1,512,128]{1,2,0:T(8,128)S(1)}, f32[1,512,128]{1,2,0:T(8,128)S(1)}, u32[]{:S(2)}, u32[]{:S(2)}) collective-permute-start(f32[1,512,128]{1,2,0:T(8,128)S(1)} %slice_bitcast_fusion.10), channel_id=1, source_target_pairs={{0,4},{4,8},{8,12},{12,16},{16,20},{20,24},{24,28},{1,5},{5,9},{9,... | collective-permute-start | bytes 786440 | tf_op jit(solution)/shard_map/ppermute | solution.py:17
  25.0 9.8 %collective-permute-start.1 = (f32[1,512,128]{1,2,0:T(8,128)S(1)}, f32[1,512,128]{1,2,0:T(8,128)S(1)}, u32[]{:S(2)}, u32[]{:S(2)}) collective-permute-start(f32[1,512,128]{1,2,0:T(8,128)S(1)} %get-tuple-element.55), channel_id=1, source_target_pairs={{4,0},{8,4},{12,8},{16,12},{20,16},{24,20},{28,24},{5,1},{9,5},{13... | collective-permute-start | bytes 786440 | tf_op jit(solution)/shard_map/ppermute | solution.py:20
  26.3 8.5 %collective-permute-start.3 = (f32[1,512,128]{1,2,0:T(8,128)S(1)}, f32[1,512,128]{1,2,0:T(8,128)S(1)}, u32[]{:S(2)}, u32[]{:S(2)}) collective-permute-start(f32[1,512,128]{1,2,0:T(8,128)S(1)} %get-tuple-element.56), channel_id=1, source_target_pairs={{1,0},{2,1},{3,2},{5,4},{6,5},{7,6},{9,8},{10,9},{11,10},{13,12},{... | collective-permute-start | bytes 786440 | tf_op jit(solution)/shard_map/ppermute | solution.py:20
  27.6 7.2 %collective-permute-start.2 = (f32[1,512,128]{1,2,0:T(8,128)S(1)}, f32[1,512,128]{1,2,0:T(8,128)S(1)}, u32[]{:S(2)}, u32[]{:S(2)}) collective-permute-start(f32[1,512,128]{1,2,0:T(8,128)S(1)} %get-tuple-element.57), channel_id=1, source_target_pairs={{0,1},{1,2},{2,3},{4,5},{5,6},{6,7},{8,9},{9,10},{10,11},{12,13},{... | collective-permute-start | bytes 786440 | tf_op jit(solution)/shard_map/ppermute | solution.py:17
  68.3 122.1 %reduce-scatter.12.cloned.1.call-start = ((), (), s32[]{:S(2)}) async-start(), calls=%async_computation.4 | async-start | bytes 163840
  93.2 7.3 %collective-permute-start.6 = (bf16[1,512,128]{1,2,0:T(8,128)(2,1)S(1)}, bf16[1,512,128]{1,2,0:T(8,128)(2,1)S(1)}, u32[]{:S(2)}, u32[]{:S(2)}) collective-permute-start(bf16[1,512,128]{1,2,0:T(8,128)(2,1)S(1)} %get-tuple-element.51), channel_id=1, source_target_pairs={{0,1},{1,2},{2,3},{4,5},{5,6},{6,7},{8,9},{9,10},{10,11},{12,13},{... | collective-permute-start | bytes 393224 | tf_op jit(solution)/shard_map/ppermute | solution.py:17
  94.5 6.0 %collective-permute-start.7 = (bf16[1,512,128]{1,2,0:T(8,128)(2,1)S(1)}, bf16[1,512,128]{1,2,0:T(8,128)(2,1)S(1)}, u32[]{:S(2)}, u32[]{:S(2)}) collective-permute-start(bf16[1,512,128]{1,2,0:T(8,128)(2,1)S(1)} %get-tuple-element.52), channel_id=1, source_target_pairs={{1,0},{2,1},{3,2},{5,4},{6,5},{7,6},{9,8},{10,9},{11,10},{13,12},{... | collective-permute-start | bytes 393224 | tf_op jit(solution)/shard_map/ppermute | solution.py:20
  95.8 6.3 %collective-permute-start.4 = (bf16[1,512,128]{1,2,0:T(8,128)(2,1)S(1)}, bf16[1,512,128]{1,2,0:T(8,128)(2,1)S(1)}, u32[]{:S(2)}, u32[]{:S(2)}) collective-permute-start(bf16[1,512,128]{1,2,0:T(8,128)(2,1)S(1)} %get-tuple-element.50), channel_id=1, source_target_pairs={{0,4},{4,8},{8,12},{12,16},{16,20},{20,24},{24,28},{1,5},{5,9},{9,... | collective-permute-start | bytes 393224 | tf_op jit(solution)/shard_map/ppermute | solution.py:17
  99.2 7.6 %collective-permute-start.5 = (bf16[1,512,128]{1,2,0:T(8,128)(2,1)S(1)}, bf16[1,512,128]{1,2,0:T(8,128)(2,1)S(1)}, u32[]{:S(2)}, u32[]{:S(2)}) collective-permute-start(bf16[1,512,128]{1,2,0:T(8,128)(2,1)S(1)} %get-tuple-element.53), channel_id=1, source_target_pairs={{4,0},{8,4},{12,8},{16,12},{20,16},{24,20},{28,24},{5,1},{9,5},{13... | collective-permute-start | bytes 393224 | tf_op jit(solution)/shard_map/ppermute | solution.py:20
  113.3 10.4 %collective-permute-start.8 = (f32[1,512,128]{1,2,0:T(8,128)S(1)}, f32[1,512,128]{1,2,0:T(8,128)S(1)}, u32[]{:S(2)}, u32[]{:S(2)}) collective-permute-start(f32[1,512,128]{1,2,0:T(8,128)S(1)} %slice_bitcast_fusion.6), channel_id=1, source_target_pairs={{0,4},{4,8},{8,12},{12,16},{16,20},{20,24},{24,28},{1,5},{5,9},{9,... | collective-permute-start | bytes 786440 | tf_op jit(solution)/shard_map/ppermute | solution.py:17
  123.8 42.6 %copy-start.11 = (f32[512,128]{0,1:T(8,128)}, f32[512,128]{0,1:T(8,128)S(1)}, u32[]{:S(2)}) copy-start(f32[512,128]{0,1:T(8,128)S(1)} %get-tuple-element.43) | copy-start | bytes 786436
  123.8 10.5 %collective-permute-start.9 = (f32[1,512,128]{1,2,0:T(8,128)S(1)}, f32[1,512,128]{1,2,0:T(8,128)S(1)}, u32[]{:S(2)}, u32[]{:S(2)}) collective-permute-start(f32[1,512,128]{1,2,0:T(8,128)S(1)} %get-tuple-element.44), channel_id=1, source_target_pairs={{4,0},{8,4},{12,8},{16,12},{20,16},{24,20},{28,24},{5,1},{9,5},{13... | collective-permute-start | bytes 786440 | tf_op jit(solution)/shard_map/ppermute | solution.py:20
  125.1 9.2 %collective-permute-start.11 = (f32[1,512,128]{1,2,0:T(8,128)S(1)}, f32[1,512,128]{1,2,0:T(8,128)S(1)}, u32[]{:S(2)}, u32[]{:S(2)}) collective-permute-start(f32[1,512,128]{1,2,0:T(8,128)S(1)} %get-tuple-element.45), channel_id=1, source_target_pairs={{1,0},{2,1},{3,2},{5,4},{6,5},{7,6},{9,8},{10,9},{11,10},{13,12},{... | collective-permute-start | bytes 786440 | tf_op jit(solution)/shard_map/ppermute | solution.py:20
  126.4 7.9 %collective-permute-start.10 = (f32[1,512,128]{1,2,0:T(8,128)S(1)}, f32[1,512,128]{1,2,0:T(8,128)S(1)}, u32[]{:S(2)}, u32[]{:S(2)}) collective-permute-start(f32[1,512,128]{1,2,0:T(8,128)S(1)} %get-tuple-element.46), channel_id=1, source_target_pairs={{0,1},{1,2},{2,3},{4,5},{5,6},{6,7},{8,9},{9,10},{10,11},{12,13},{... | collective-permute-start | bytes 786440 | tf_op jit(solution)/shard_map/ppermute | solution.py:17
  134.5 31.9 %copy-start.6 = (f32[512,128]{0,1:T(8,128)}, f32[512,128]{0,1:T(8,128)S(1)}, u32[]{:S(2)}) copy-start(f32[512,128]{0,1:T(8,128)S(1)} %get-tuple-element.49) | copy-start | bytes 786436
  167.4 114.2 %reduce-scatter.14.cloned.1.call-start = ((), (), s32[]{:S(2)}) async-start(), calls=%async_computation.5 | async-start | bytes 163840
  191.6 7.3 %collective-permute-start.14 = (bf16[1,512,128]{1,2,0:T(8,128)(2,1)S(1)}, bf16[1,512,128]{1,2,0:T(8,128)(2,1)S(1)}, u32[]{:S(2)}, u32[]{:S(2)}) collective-permute-start(bf16[1,512,128]{1,2,0:T(8,128)(2,1)S(1)} %get-tuple-element.40), channel_id=1, source_target_pairs={{0,1},{1,2},{2,3},{4,5},{5,6},{6,7},{8,9},{9,10},{10,11},{12,13},{... | collective-permute-start | bytes 393224 | tf_op jit(solution)/shard_map/ppermute | solution.py:17
  192.9 6.0 %collective-permute-start.15 = (bf16[1,512,128]{1,2,0:T(8,128)(2,1)S(1)}, bf16[1,512,128]{1,2,0:T(8,128)(2,1)S(1)}, u32[]{:S(2)}, u32[]{:S(2)}) collective-permute-start(bf16[1,512,128]{1,2,0:T(8,128)(2,1)S(1)} %get-tuple-element.41), channel_id=1, source_target_pairs={{1,0},{2,1},{3,2},{5,4},{6,5},{7,6},{9,8},{10,9},{11,10},{13,12},{... | collective-permute-start | bytes 393224 | tf_op jit(solution)/shard_map/ppermute | solution.py:20
  194.2 6.3 %collective-permute-start.12 = (bf16[1,512,128]{1,2,0:T(8,128)(2,1)S(1)}, bf16[1,512,128]{1,2,0:T(8,128)(2,1)S(1)}, u32[]{:S(2)}, u32[]{:S(2)}) collective-permute-start(bf16[1,512,128]{1,2,0:T(8,128)(2,1)S(1)} %get-tuple-element.39), channel_id=1, source_target_pairs={{0,4},{4,8},{8,12},{12,16},{16,20},{20,24},{24,28},{1,5},{5,9},{9,... | collective-permute-start | bytes 393224 | tf_op jit(solution)/shard_map/ppermute | solution.py:17
  197.6 7.7 %collective-permute-start.13 = (bf16[1,512,128]{1,2,0:T(8,128)(2,1)S(1)}, bf16[1,512,128]{1,2,0:T(8,128)(2,1)S(1)}, u32[]{:S(2)}, u32[]{:S(2)}) collective-permute-start(bf16[1,512,128]{1,2,0:T(8,128)(2,1)S(1)} %get-tuple-element.42), channel_id=1, source_target_pairs={{4,0},{8,4},{12,8},{16,12},{20,16},{24,20},{28,24},{5,1},{9,5},{13... | collective-permute-start | bytes 393224 | tf_op jit(solution)/shard_map/ppermute | solution.py:20
  212.3 84.2 %copy-start.3 = (f32[512,128]{0,1:T(8,128)S(1)}, f32[512,128]{0,1:T(8,128)}, u32[]{:S(2)}) copy-start(f32[512,128]{0,1:T(8,128)} %copy-done.2) | copy-start | bytes 786436
  212.4 16.0 %collective-permute-start.16 = (f32[1,512,128]{1,2,0:T(8,128)S(1)}, f32[1,512,128]{1,2,0:T(8,128)S(1)}, u32[]{:S(2)}, u32[]{:S(2)}) collective-permute-start(f32[1,512,128]{1,2,0:T(8,128)S(1)} %get-tuple-element.35), channel_id=1, source_target_pairs={{0,4},{4,8},{8,12},{12,16},{16,20},{20,24},{24,28},{1,5},{5,9},{9,... | collective-permute-start | bytes 786440 | tf_op jit(solution)/shard_map/ppermute | solution.py:17
  216.7 11.8 %collective-permute-start.17 = (f32[1,512,128]{1,2,0:T(8,128)S(1)}, f32[1,512,128]{1,2,0:T(8,128)S(1)}, u32[]{:S(2)}, u32[]{:S(2)}) collective-permute-start(f32[1,512,128]{1,2,0:T(8,128)S(1)} %get-tuple-element.36), channel_id=1, source_target_pairs={{4,0},{8,4},{12,8},{16,12},{20,16},{24,20},{28,24},{5,1},{9,5},{13... | collective-permute-start | bytes 786440 | tf_op jit(solution)/shard_map/ppermute | solution.py:20
  218.0 10.5 %collective-permute-start.19 = (f32[1,512,128]{1,2,0:T(8,128)S(1)}, f32[1,512,128]{1,2,0:T(8,128)S(1)}, u32[]{:S(2)}, u32[]{:S(2)}) collective-permute-start(f32[1,512,128]{1,2,0:T(8,128)S(1)} %get-tuple-element.37), channel_id=1, source_target_pairs={{1,0},{2,1},{3,2},{5,4},{6,5},{7,6},{9,8},{10,9},{11,10},{13,12},{... | collective-permute-start | bytes 786440 | tf_op jit(solution)/shard_map/ppermute | solution.py:20
  219.3 9.2 %collective-permute-start.18 = (f32[1,512,128]{1,2,0:T(8,128)S(1)}, f32[1,512,128]{1,2,0:T(8,128)S(1)}, u32[]{:S(2)}, u32[]{:S(2)}) collective-permute-start(f32[1,512,128]{1,2,0:T(8,128)S(1)} %get-tuple-element.38), channel_id=1, source_target_pairs={{0,1},{1,2},{2,3},{4,5},{5,6},{6,7},{8,9},{9,10},{10,11},{12,13},{... | collective-permute-start | bytes 786440 | tf_op jit(solution)/shard_map/ppermute | solution.py:17
  282.8 7.3 %collective-permute-start.22 = (bf16[1,512,128]{1,2,0:T(8,128)(2,1)S(1)}, bf16[1,512,128]{1,2,0:T(8,128)(2,1)S(1)}, u32[]{:S(2)}, u32[]{:S(2)}) collective-permute-start(bf16[1,512,128]{1,2,0:T(8,128)(2,1)S(1)} %get-tuple-element.26), channel_id=1, source_target_pairs={{0,1},{1,2},{2,3},{4,5},{5,6},{6,7},{8,9},{9,10},{10,11},{12,13},{... | collective-permute-start | bytes 393224 | tf_op jit(solution)/shard_map/ppermute | solution.py:17
  284.1 6.0 %collective-permute-start.23 = (bf16[1,512,128]{1,2,0:T(8,128)(2,1)S(1)}, bf16[1,512,128]{1,2,0:T(8,128)(2,1)S(1)}, u32[]{:S(2)}, u32[]{:S(2)}) collective-permute-start(bf16[1,512,128]{1,2,0:T(8,128)(2,1)S(1)} %get-tuple-element.27), channel_id=1, source_target_pairs={{1,0},{2,1},{3,2},{5,4},{6,5},{7,6},{9,8},{10,9},{11,10},{13,12},{... | collective-permute-start | bytes 393224 | tf_op jit(solution)/shard_map/ppermute | solution.py:20
  285.4 6.3 %collective-permute-start.20 = (bf16[1,512,128]{1,2,0:T(8,128)(2,1)S(1)}, bf16[1,512,128]{1,2,0:T(8,128)(2,1)S(1)}, u32[]{:S(2)}, u32[]{:S(2)}) collective-permute-start(bf16[1,512,128]{1,2,0:T(8,128)(2,1)S(1)} %get-tuple-element.25), channel_id=1, source_target_pairs={{0,4},{4,8},{8,12},{12,16},{16,20},{20,24},{24,28},{1,5},{5,9},{9,... | collective-permute-start | bytes 393224 | tf_op jit(solution)/shard_map/ppermute | solution.py:17
  288.8 7.6 %collective-permute-start.21 = (bf16[1,512,128]{1,2,0:T(8,128)(2,1)S(1)}, bf16[1,512,128]{1,2,0:T(8,128)(2,1)S(1)}, u32[]{:S(2)}, u32[]{:S(2)}) collective-permute-start(bf16[1,512,128]{1,2,0:T(8,128)(2,1)S(1)} %get-tuple-element.28), channel_id=1, source_target_pairs={{4,0},{8,4},{12,8},{16,12},{20,16},{24,20},{28,24},{5,1},{9,5},{13... | collective-permute-start | bytes 393224 | tf_op jit(solution)/shard_map/ppermute | solution.py:20
  (7 other events, 52.4 us)
Sparse Core Ops, SparseCore 0:
  68.4 23.4 reduce-scatter.9
  167.6 22.7 reduce-scatter.11
  263.0 18.5 reduce-scatter.13
where the time goes:
time: 308 us; the launch traced here: 307 us
  waiting for transfers between devices  111 us (36%)
  blocking collectives  94.8 us (31%)
  starting transfers between devices  52.2 us (17%)
  matrix products  22 us (7%)
  between operations  13.7 us (4%)
  local copies, waits for them, and re-layouts  8.81 us (3%)
  other arithmetic  4.11 us (1%)
    all_gather x3, blocking collectives, local(): lax.all_gather(coarse_in, 'sx', axis=0, tiled=True)  94.8 us
    unnamed x6, waiting for transfers between devices  65.3 us
    ppermute x12, starting transfers between devices, with_halo(): lax.ppermute(lax.slice_in_dim(block, block.shape[dim] - width, None, axis...  36.6 us
    ppermute x12, waiting for transfers between devices, with_halo(): lax.ppermute(lax.slice_in_dim(block, 0, width, axis=dim), axis, backward)  23.2 us
    ppermute x12, waiting for transfers between devices, with_halo(): lax.ppermute(lax.slice_in_dim(block, block.shape[dim] - width, None, axis...  22.4 us
    dot_general x3, matrix products, local(): jnp.dot(operator, multipliers.astype(jnp.bfloat16), preferred_element_typ...  19.5 us
    ppermute x12, starting transfers between devices, with_halo(): lax.ppermute(lax.slice_in_dim(block, 0, width, axis=dim), axis, backward)  15.5 us
    unnamed x31, local copies, waits for them, and re-layouts  7.18 us
  transfers between devices with their start and end apart: 27, of which 14 were waited for; matrix products, arithmetic and copies ran while one was open for 0% of the time, Pallas kernels for 0%

commit v1 on v0

v1 whole, which is shorter than its diff:
```python
import functools

import jax
import jax.numpy as jnp
from jax import lax
from jax.experimental import pallas as pl
from jax.experimental.pallas import tpu as pltpu
from jax.sharding import PartitionSpec as P

ITERS = 3
DAMPING = 0.5
MESH = pl.DeviceIdType.MESH
F32 = jnp.float32
BF16 = jnp.bfloat16


def iterate(
    nx,
    ny,
    dual_hbm,
    loads,
    basis,
    tile,
    out,
    dual,
    faces,
    halo,
    beside_basis,
    spread,
    half,
    resid,
    gathered,
    slices,
    arrived,
    coarse,
    coarse_near,
    dual_sem,
    face_send,
    face_recv,
    basis_send,
    basis_recv,
    gather_send,
    gather_recv,
    slice_send,
    slice_recv,
    near_send,
    near_recv,
):
    a, b = lax.axis_index("sx"), lax.axis_index("sy")
    width = loads.shape[0] // 4
    modes = basis.shape[0]
    peers = ((a - 1, b), (a + 1, b), (a, b - 1), (a, b + 1))
    present = (a > 0, a < nx - 1, b > 0, b < ny - 1)
    opposite = (1, 0, 3, 2)

    dual_copy = pltpu.make_async_copy(dual_hbm, dual, dual_sem)
    dual_copy.start()

    barrier = pltpu.get_barrier_semaphore()
    for k in range(1, nx):
        pl.semaphore_signal(
            barrier, inc=1, device_id=(lax.rem(a + k, nx), b), device_id_type=MESH
        )
    for k in range(1, ny):
        pl.semaphore_signal(
            barrier, inc=1, device_id=(a, lax.rem(b + k, ny)), device_id_type=MESH
        )

    def rows(f):
        return pl.ds(f * width, width)

    for f in range(4):
        faces[0, f] = loads[rows(f), :].astype(BF16)

        @pl.when(jnp.logical_not(present[f]))
        def _():
            for step in range(ITERS):
                halo[step, f] = jnp.zeros(halo.shape[2:], BF16)
                coarse_near[step, f] = jnp.zeros(coarse_near.shape[2:], BF16)
            beside_basis[f] = jnp.zeros(beside_basis.shape[1:], BF16)

    pl.semaphore_wait(barrier, nx - 1 + ny - 1)

    def face_copy(step, f, slot):
        return pltpu.make_async_remote_copy(
            src_ref=faces.at[step, f],
            dst_ref=halo.at[step, slot],
            send_sem=face_send.at[step, f],
            recv_sem=face_recv.at[step, slot],
            device_id=peers[f],
            device_id_type=MESH,
        )

    def basis_copy(f, slot):
        return pltpu.make_async_remote_copy(
            src_ref=basis.at[:, rows(f)],
            dst_ref=beside_basis.at[slot],
            send_sem=basis_send.at[f],
            recv_sem=basis_recv.at[slot],
            device_id=peers[f],
            device_id_type=MESH,
        )

    def near_copy(step, f, slot):
        return pltpu.make_async_remote_copy(
            src_ref=coarse.at[step],
            dst_ref=coarse_near.at[step, slot],
            send_sem=near_send.at[step, f],
            recv_sem=near_recv.at[step, slot],
            device_id=peers[f],
            device_id_type=MESH,
        )

    def gather_copy(step, k):
        return pltpu.make_async_remote_copy(
            src_ref=gathered.at[step, a],
            dst_ref=gathered.at[step, a],
            send_sem=gather_send.at[step, k],
            recv_sem=gather_recv.at[step, k],
            device_id=(lax.rem(a + k, nx), b),
            device_id_type=MESH,
        )

    def slice_copy(step, k):
        target = lax.rem(b + k, ny)
        return pltpu.make_async_remote_copy(
            src_ref=slices.at[step, target],
            dst_ref=arrived.at[step, k],
            send_sem=slice_send.at[step, k],
            recv_sem=slice_recv.at[step, k],
            device_id=(a, target),
            device_id_type=MESH,
        )

    def each(make, f, what):
        @pl.when(present[f])
        def _():
            getattr(make(f, opposite[f]), what)()

    def expect(make, f):
        @pl.when(present[f])
        def _():
            make(f, f).wait_recv()

    for step in range(ITERS):
        here = functools.partial(face_copy, step)
        near = functools.partial(near_copy, step)
        for f in range(4):
            if step:

                @pl.loop(0, 2)
                def _(part):
                    span = width // 2
                    start = pl.multiple_of(f * width + part * span, span)
                    local = loads[pl.ds(start, span), :] - jnp.dot(
                        dual[pl.ds(start, span), :], half[...], preferred_element_type=F32
                    )
                    resid[pl.ds(start, span), :] = local
                    inner = pl.multiple_of(part * span, span)
                    faces[step, f, pl.ds(inner, span), :] = local.astype(BF16)

            each(here, f, "start")
        if step == 0:
            for f in range(4):
                each(basis_copy, f, "start")
        total = jnp.zeros((modes, loads.shape[1]), F32)
        for f in range(4):
            expect(here, f)
            own = resid if step else loads
            value = own[rows(f), :] - halo[step, f].astype(F32)
            resid[rows(f), :] = value
            total += jnp.dot(
                basis[:, rows(f)], value.astype(BF16), preferred_element_type=F32
            )
        gathered[step, a] = total.astype(BF16)
        for k in range(1, nx):
            gather_copy(step, k).start()
        if step == 0:
            dual_copy.wait()
            for f in range(4):
                expect(basis_copy, f)
                pair = jnp.concatenate([basis[:, rows(f)], -beside_basis[f]], axis=0)
                spread[rows(f), :] = pair.astype(F32).T.astype(BF16)
        for k in range(1, nx):
            gather_copy(step, k).wait_recv()
        column = gathered[step].reshape(nx * modes, loads.shape[1])
        partial = jnp.dot(tile[...], column, preferred_element_type=F32)
        slices[step] = partial.reshape(ny, modes, loads.shape[1])
        for k in range(1, ny):
            slice_copy(step, k).start()
        total = slices[step, b]
        for k in range(1, ny):
            slice_copy(step, k).wait_recv()
            total += arrived[step, k]
        coarse[step] = total.astype(BF16)
        for f in range(4):
            each(near, f, "start")
        for f in range(4):
            expect(near, f)
            stacked = jnp.concatenate([coarse[step], coarse_near[step, f]], axis=0)
            correction = jnp.dot(spread[rows(f), :], stacked, preferred_element_type=F32)
            value = DAMPING * (resid[rows(f), :] - correction)
            if step:
                value += out[rows(f), :]
            out[rows(f), :] = value
            if step < ITERS - 1:
                half[rows(f), :] = value.astype(BF16)

    for f in range(4):
        each(basis_copy, f, "wait_send")
        for step in range(ITERS):
            each(functools.partial(face_copy, step), f, "wait_send")
            each(functools.partial(near_copy, step), f, "wait_send")
    for step in range(ITERS):
        for k in range(1, nx):
            gather_copy(step, k).wait_send()
        for k in range(1, ny):
            slice_copy(step, k).wait_send()


def local(nx, ny, dual_ops, loads, kernel_basis, coarse_inverse):
    n, cols = loads.shape[2:]
    modes = kernel_basis.shape[2]
    width = n // 4
    vmem = pl.BlockSpec(memory_space=pltpu.VMEM)
    dma = pltpu.SemaphoreType.DMA
    result = pl.pallas_call(
        functools.partial(iterate, nx, ny),
        out_shape=jax.ShapeDtypeStruct((n, cols), F32),
        in_specs=[pl.BlockSpec(memory_space=pl.ANY), vmem, vmem, vmem],
        out_specs=vmem,
        scratch_shapes=[
            pltpu.VMEM((n, n), BF16),
            pltpu.VMEM((ITERS, 4, width, cols), BF16),
            pltpu.VMEM((ITERS, 4, width, cols), BF16),
            pltpu.VMEM((4, modes, width), BF16),
            pltpu.VMEM((n, 2 * modes), BF16),
            pltpu.VMEM((n, cols), BF16),
            pltpu.VMEM((n, cols), F32),
            pltpu.VMEM((ITERS, nx, modes, cols), BF16),
            pltpu.VMEM((ITERS, ny, modes, cols), F32),
            pltpu.VMEM((ITERS, ny, modes, cols), F32),
            pltpu.VMEM((ITERS, modes, cols), BF16),
            pltpu.VMEM((ITERS, 4, modes, cols), BF16),
            dma(()),
            dma((ITERS, 4)),
            dma((ITERS, 4)),
            dma((4,)),
            dma((4,)),
            dma((ITERS, nx)),
            dma((ITERS, nx)),
            dma((ITERS, ny)),
            dma((ITERS, ny)),
            dma((ITERS, 4)),
            dma((ITERS, 4)),
        ],
        compiler_params=pltpu.CompilerParams(
            collective_id=0, has_side_effects=True, vmem_limit_bytes=40 * 2**20
        ),
    )(dual_ops[0, 0], loads[0, 0], kernel_basis[0, 0], coarse_inverse[0, 0])
    return result[None, None]


def solution(mesh):
    placed = P("sx", "sy", None, None)
    return jax.shard_map(
        functools.partial(local, mesh.shape["sx"], mesh.shape["sy"]),
        mesh=mesh,
        in_specs=(placed,) * 4,
        out_specs=placed,
        check_vma=False,
    )
```

time: 308 us -> 76.2 us (0.25)
  waiting for transfers between devices: 111 us -> 0 us
  blocking collectives: 94.8 us -> 0 us
  Pallas kernels: 0 us -> 68.4 us
  starting transfers between devices: 52.2 us -> 0 us
  matrix products: 22 us -> 0 us
  between operations: 13.7 us -> 0.01 us
  other arithmetic: 4.11 us -> 0 us
    all_gather x3 -> x0, blocking collectives: 94.8 us -> none  [local(): lax.all_gather(coarse_in, 'sx', axis=0, tiled=True)]
    pallas_call x0 -> x1, Pallas kernels: none -> 68.4 us  [local(): pl.pallas_call(functools.partial(iterate, nx, ny), out_shape=jax.ShapeDty...]
    unnamed x6 -> x0, waiting for transfers between devices: 65.3 us -> none
    ppermute x24 -> x0, starting transfers between devices: 52.1 us -> none  [the longest x12 36.6 us: with_halo(): lax.ppermute(lax.slice_in_dim(block, block.shape[dim] - width, None, axis...]
    ppermute x24 -> x0, waiting for transfers between devices: 45.6 us -> none  [the longest x12 23.2 us: with_halo(): lax.ppermute(lax.slice_in_dim(block, 0, width, axis=dim), axis, backward)]
    dot_general x12 -> x0, matrix products: 22 us -> none  [the longest x3 19.5 us: local(): jnp.dot(operator, multipliers.astype(jnp.bfloat16), preferred_element_typ...]
    unnamed x31 -> x9, local copies, waits for them, and re-layouts: 7.18 us -> 7.48 us
  transfers between devices with their start and end apart: 27 -> 0, of which waited for: 14 -> 0; matrix products, arithmetic and copies ran while one was open for 0% -> 0% of each run, Pallas kernels for 0% -> 0%
where the time goes in v1:
time: 76.2 us; the launch traced here: 75.9 us
  Pallas kernels  68.4 us (90%)
  local copies, waits for them, and re-layouts  7.48 us (10%)
    pallas_call x1, Pallas kernels, local(): pl.pallas_call(functools.partial(iterate, nx, ny), out_shape=jax.ShapeDty...  68.4 us
    unnamed x9, local copies, waits for them, and re-layouts  7.48 us

profile of v1, /device:TPU:0, one launch (start us, length us, event | category | flops | bytes accessed | tf_op | source)
XLA Modules:
  0.0 75.9 jit_solution(11331490523515544795)
XLA Ops:
  0.0 0.0 copy-start
  0.0 3.4 %copy-done = bf16[1,1,2048,2048]{3,2,1,0:T(8,128)(2,1)S(1)} copy-done((bf16[1,1,2048,2048]{3,2,1,0:T(8,128)(2,1)S(1)}, bf16[1,1,2048,2048]{3,2,1,0:T(8,128)(2,1)}, u32[]{:S(2)}) %copy-start) | copy-done | bytes 8388632
  3.4 0.0 copy-start.1
  3.4 1.2 %copy-done.1 = f32[1,1,2048,128]{3,2,1,0:T(8,128)S(1)} copy-done((f32[1,1,2048,128]{3,2,1,0:T(8,128)S(1)}, f32[1,1,2048,128]{3,2,1,0:T(8,128)}, u32[]{:S(2)}) %copy-start.1) | copy-done | bytes 1048600
  4.6 0.0 copy-start.2
  4.6 0.9 %copy-done.2 = bf16[1,1,64,2048]{3,2,1,0:T(8,128)(2,1)S(1)} copy-done((bf16[1,1,64,2048]{3,2,1,0:T(8,128)(2,1)S(1)}, bf16[1,1,64,2048]{3,2,1,0:T(8,128)(2,1)}, u32[]{:S(2)}) %copy-start.2) | copy-done | bytes 262168
  5.6 0.0 copy-start.3
  5.6 0.9 %copy-done.3 = bf16[1,1,256,512]{3,2,1,0:T(8,128)(2,1)S(1)} copy-done((bf16[1,1,256,512]{3,2,1,0:T(8,128)(2,1)S(1)}, bf16[1,1,256,512]{3,2,1,0:T(8,128)(2,1)}, u32[]{:S(2)}) %copy-start.3) | copy-done | bytes 262168
  6.5 68.4 %shard_map.46 = f32[2048,128]{1,0:T(8,128)S(1)} custom-call(bf16[2048,2048]{1,0:T(8,128)(2,1)S(1)} %bitcast.5, f32[2048,128]{1,0:T(8,128)S(1)} %bitcast.7, bf16[64,2048]{1,0:T(8,128)(2,1)S(1)} %bitcast.8, bf16[256,512]{1,0:T(8,128)(2,1)S(1)} %bitcast.9), custom_call_target="tpu_custom_call" | custom-call | tf_op jit(solution)/shard_map/pallas_call | solution.py:227
  75.0 1.0 %copy.6 = f32[1,1,2048,128]{3,2,1,0:T(8,128)} copy(f32[1,1,2048,128]{3,2,1,0:T(8,128)S(1)} %bitcast.6) | data formatting | bytes 2097152
Async XLA Ops:
  0.0 3.4 %copy-start = (bf16[1,1,2048,2048]{3,2,1,0:T(8,128)(2,1)S(1)}, bf16[1,1,2048,2048]{3,2,1,0:T(8,128)(2,1)}, u32[]{:S(2)}) copy-start(bf16[1,1,2048,2048]{3,2,1,0:T(8,128)(2,1)} %param.4) | copy-start | bytes 25165828
  3.4 1.2 %copy-start.1 = (f32[1,1,2048,128]{3,2,1,0:T(8,128)S(1)}, f32[1,1,2048,128]{3,2,1,0:T(8,128)}, u32[]{:S(2)}) copy-start(f32[1,1,2048,128]{3,2,1,0:T(8,128)} %param.5) | copy-start | bytes 3145732
  4.6 0.9 %copy-start.2 = (bf16[1,1,64,2048]{3,2,1,0:T(8,128)(2,1)S(1)}, bf16[1,1,64,2048]{3,2,1,0:T(8,128)(2,1)}, u32[]{:S(2)}) copy-start(bf16[1,1,64,2048]{3,2,1,0:T(8,128)(2,1)} %param.6) | copy-start | bytes 786436
  5.6 0.9 %copy-start.3 = (bf16[1,1,256,512]{3,2,1,0:T(8,128)(2,1)S(1)}, bf16[1,1,256,512]{3,2,1,0:T(8,128)(2,1)}, u32[]{:S(2)}) copy-start(bf16[1,1,256,512]{3,2,1,0:T(8,128)(2,1)} %param.7) | copy-start | bytes 786436

commit v2 on v1

v2 whole, which is shorter than its diff:
```python
import functools

import jax
import jax.numpy as jnp
from jax import lax
from jax.experimental import pallas as pl
from jax.experimental.pallas import tpu as pltpu
from jax.sharding import PartitionSpec as P

ITERS = 3
DAMPING = 0.5
MESH = pl.DeviceIdType.MESH
F32 = jnp.float32
BF16 = jnp.bfloat16


def iterate(
    nx,
    ny,
    dual_hbm,
    loads_hbm,
    basis_hbm,
    tile_hbm,
    out,
    dual,
    loads,
    basis,
    tile,
    faces,
    halo,
    beside_basis,
    spread,
    spread_rows,
    image,
    gram,
    half,
    resid,
    base,
    base_modes,
    offered,
    offers,
    gathered,
    slices,
    arrived,
    coarse,
    coarse_near,
    local_sem,
    face_send,
    face_recv,
    basis_send,
    basis_recv,
    offer_send,
    offer_recv,
    gather_send,
    gather_recv,
    slice_send,
    slice_recv,
    near_send,
    near_recv,
):
    a, b = lax.axis_index("sx"), lax.axis_index("sy")
    n, cols = loads.shape
    width = n // 4
    modes = basis.shape[0]
    peers = ((a - 1, b), (a + 1, b), (a, b - 1), (a, b + 1))
    present = (a > 0, a < nx - 1, b > 0, b < ny - 1)
    opposite = (1, 0, 3, 2)

    loads_copy = pltpu.make_async_copy(loads_hbm, loads, local_sem.at[0])
    basis_load = pltpu.make_async_copy(basis_hbm, basis, local_sem.at[1])
    dual_copy = pltpu.make_async_copy(dual_hbm, dual, local_sem.at[2])
    tile_copy = pltpu.make_async_copy(tile_hbm, tile, local_sem.at[3])
    loads_copy.start()
    basis_load.start()
    dual_copy.start()
    tile_copy.start()

    barrier = pltpu.get_barrier_semaphore()
    for k in range(1, nx):
        pl.semaphore_signal(
            barrier, inc=1, device_id=(lax.rem(a + k, nx), b), device_id_type=MESH
        )
    for k in range(1, ny):
        pl.semaphore_signal(
            barrier, inc=1, device_id=(a, lax.rem(b + k, ny)), device_id_type=MESH
        )

    def rows(f):
        return pl.ds(f * width, width)

    for f in range(4):

        @pl.when(jnp.logical_not(present[f]))
        def _():
            for step in range(ITERS):
                halo[step, f] = jnp.zeros(halo.shape[2:], BF16)
                coarse_near[step, f] = jnp.zeros(coarse_near.shape[2:], BF16)
                offers[step, f] = jnp.zeros(offers.shape[2:], BF16)
            beside_basis[f] = jnp.zeros(beside_basis.shape[1:], BF16)

    loads_copy.wait()
    for f in range(4):
        faces[0, f] = loads[rows(f), :].astype(BF16)
    basis_load.wait()

    pl.semaphore_wait(barrier, nx - 1 + ny - 1)

    def to_face(src, dst, sends, recvs, f, slot):
        return pltpu.make_async_remote_copy(
            src_ref=src,
            dst_ref=dst,
            send_sem=sends,
            recv_sem=recvs,
            device_id=peers[f],
            device_id_type=MESH,
        )

    def face_copy(step, f, slot):
        return to_face(
            faces.at[step, f],
            halo.at[step, slot],
            face_send.at[step, f],
            face_recv.at[step, slot],
            f,
            slot,
        )

    def basis_copy(step, f, slot):
        return to_face(
            basis.at[:, rows(f)],
            beside_basis.at[slot],
            basis_send.at[f],
            basis_recv.at[slot],
            f,
            slot,
        )

    def offer_copy(step, f, slot):
        return to_face(
            offered.at[step, f],
            offers.at[step, slot],
            offer_send.at[step, f],
            offer_recv.at[step, slot],
            f,
            slot,
        )

    def near_copy(step, f, slot):
        return to_face(
            coarse.at[step],
            coarse_near.at[step, slot],
            near_send.at[step, f],
            near_recv.at[step, slot],
            f,
            slot,
        )

    def gather_copy(step, k):
        return pltpu.make_async_remote_copy(
            src_ref=gathered.at[step, a],
            dst_ref=gathered.at[step, a],
            send_sem=gather_send.at[step, k],
            recv_sem=gather_recv.at[step, k],
            device_id=(lax.rem(a + k, nx), b),
            device_id_type=MESH,
        )

    def slice_copy(step, k):
        target = lax.rem(b + k, ny)
        return pltpu.make_async_remote_copy(
            src_ref=slices.at[step, target],
            dst_ref=arrived.at[step, k],
            send_sem=slice_send.at[step, k],
            recv_sem=slice_recv.at[step, k],
            device_id=(a, target),
            device_id_type=MESH,
        )

    def send(make, step, f):
        @pl.when(present[f])
        def _():
            make(step, f, opposite[f]).start()

    def sent(make, step, f):
        @pl.when(present[f])
        def _():
            make(step, f, opposite[f]).wait_send()

    def expect(make, step, f):
        @pl.when(present[f])
        def _():
            make(step, f, f).wait_recv()

    def dot(x, y):
        return jnp.dot(x, y, preferred_element_type=F32)

    def with_near(step):
        return jnp.concatenate([coarse[step]] + [coarse_near[step, f] for f in range(4)], axis=0)

    def share(step, total):
        gathered[step, a] = total.astype(BF16)
        for k in range(1, nx):
            gather_copy(step, k).start()

    def spread_tiles(step):
        for k in range(1, nx):
            gather_copy(step, k).wait_recv()
        partial = dot(tile[...], gathered[step].reshape(nx * modes, cols))
        slices[step] = partial.astype(BF16).reshape(ny, modes, cols)
        for k in range(1, ny):
            slice_copy(step, k).start()

    def finish_coarse(step):
        total = slices[step, b].astype(F32)
        for k in range(1, ny):
            slice_copy(step, k).wait_recv()
            total += arrived[step, k].astype(F32)
        coarse[step] = total.astype(BF16)
        for f in range(4):
            send(near_copy, step, f)

    def apply_dual(first, count):
        span = width // 2

        @pl.loop(first, first + count)
        def _(part):
            start = pl.multiple_of(part * span, span)
            base[pl.ds(start, span), :] = loads[pl.ds(start, span), :] - dot(
                dual[pl.ds(start, span), :], half[...]
            )

    def to_modes(read):
        own = jnp.zeros((modes, cols), F32)
        for f in range(4):
            both = dot(spread_rows[f], read(f).astype(BF16))
            own += both[:modes]
            base_modes[pl.ds((f + 1) * modes, modes), :] = both[modes:]
        base_modes[pl.ds(0, modes), :] = own

    def correct(step, f):
        stacked = jnp.concatenate([coarse[step], coarse_near[step, f]], axis=0)
        return DAMPING * dot(spread[rows(f), :], stacked)

    for f in range(4):
        send(face_copy, 0, f)
    for f in range(4):
        send(basis_copy, 0, f)
    total = jnp.zeros((modes, cols), F32)
    for f in range(4):
        expect(face_copy, 0, f)
        value = loads[rows(f), :] - halo[0, f].astype(F32)
        total += dot(basis[:, rows(f)], value.astype(BF16))
        out[rows(f), :] = DAMPING * value
        half[rows(f), :] = (DAMPING * value).astype(BF16)
    share(0, total)
    for f in range(4):
        expect(basis_copy, 0, f)
        pair = jnp.concatenate([basis[:, rows(f)], -beside_basis[f]], axis=0)
        spread_rows[f] = pair
        spread[rows(f), :] = pair.astype(F32).T.astype(BF16)
    dual_copy.wait()
    tile_copy.wait()
    spread_tiles(0)

    @pl.loop(0, 8)
    def _(part):
        span = width // 2
        start = pl.multiple_of(part * span, span)
        own = jnp.zeros((span, modes), F32)
        columns = []
        for f in range(4):
            both = dot(dual[pl.ds(start, span), rows(f)], spread[rows(f), :])
            own += both[:, :modes]
            columns.append(both[:, modes:])
        image[pl.ds(start, span), :] = jnp.concatenate([own] + columns, axis=1).astype(BF16)

    finish_coarse(0)
    own = jnp.zeros((modes, 5 * modes), F32)
    for f in range(4):
        both = dot(spread_rows[f], image[rows(f), :])
        own += both[:modes]
        gram[pl.ds((f + 1) * modes, modes), :] = both[modes:].astype(BF16)
    gram[pl.ds(0, modes), :] = own.astype(BF16)
    apply_dual(0, 8)
    to_modes(lambda f: base[rows(f), :])

    for step in range(1, ITERS):
        for f in range(4):
            expect(near_copy, step - 1, f)
        stack = with_near(step - 1)
        total_modes = base_modes[...] + DAMPING * dot(gram[...], stack)
        for f in range(4):
            offered[step, f] = total_modes[(f + 1) * modes : (f + 2) * modes].astype(BF16)
            send(offer_copy, step, f)
        for f in range(4):
            value = base[rows(f), :] + DAMPING * dot(image[rows(f), :], stack)
            resid[rows(f), :] = value
            faces[step, f] = value.astype(BF16)
            send(face_copy, step, f)
        total = total_modes[:modes]
        for f in range(4):
            expect(offer_copy, step, f)
            total += offers[step, f].astype(F32)
        share(step, total)
        for f in range(4):
            out[rows(f), :] = out[rows(f), :] - correct(step - 1, f)
        spread_tiles(step)
        for f in range(4):
            expect(face_copy, step, f)
            value = out[rows(f), :] + DAMPING * (resid[rows(f), :] - halo[step, f].astype(F32))
            out[rows(f), :] = value
            if step < ITERS - 1:
                half[rows(f), :] = value.astype(BF16)
        if step < ITERS - 1:
            apply_dual(0, 4)
        finish_coarse(step)
        if step < ITERS - 1:
            apply_dual(4, 4)
            to_modes(lambda f: base[rows(f), :])

    for f in range(4):
        expect(near_copy, ITERS - 1, f)
        out[rows(f), :] = out[rows(f), :] - correct(ITERS - 1, f)

    for f in range(4):
        sent(basis_copy, 0, f)
        for step in range(ITERS):
            sent(face_copy, step, f)
            sent(near_copy, step, f)
            if step:
                sent(offer_copy, step, f)
    for step in range(ITERS):
        for k in range(1, nx):
            gather_copy(step, k).wait_send()
        for k in range(1, ny):
            slice_copy(step, k).wait_send()


def local(nx, ny, dual_ops, loads, kernel_basis, coarse_inverse):
    n, cols = loads.shape[2:]
    modes = kernel_basis.shape[2]
    width = n // 4
    dma = pltpu.SemaphoreType.DMA
    result = pl.pallas_call(
        functools.partial(iterate, nx, ny),
        out_shape=jax.ShapeDtypeStruct((n, cols), F32),
        in_specs=[pl.BlockSpec(memory_space=pl.ANY)] * 4,
        out_specs=pl.BlockSpec(memory_space=pltpu.VMEM),
        scratch_shapes=[
            pltpu.VMEM((n, n), BF16),
            pltpu.VMEM((n, cols), F32),
            pltpu.VMEM((modes, n), BF16),
            pltpu.VMEM(coarse_inverse.shape[2:], BF16),
            pltpu.VMEM((ITERS, 4, width, cols), BF16),
            pltpu.VMEM((ITERS, 4, width, cols), BF16),
            pltpu.VMEM((4, modes, width), BF16),
            pltpu.VMEM((n, 2 * modes), BF16),
            pltpu.VMEM((4, 2 * modes, width), BF16),
            pltpu.VMEM((n, 5 * modes), BF16),
            pltpu.VMEM((5 * modes, 5 * modes), BF16),
            pltpu.VMEM((n, cols), BF16),
            pltpu.VMEM((n, cols), F32),
            pltpu.VMEM((n, cols), F32),
            pltpu.VMEM((5 * modes, cols), F32),
            pltpu.VMEM((ITERS, 4, modes, cols), BF16),
            pltpu.VMEM((ITERS, 4, modes, cols), BF16),
            pltpu.VMEM((ITERS, nx, modes, cols), BF16),
            pltpu.VMEM((ITERS, ny, modes, cols), BF16),
            pltpu.VMEM((ITERS, ny, modes, cols), BF16),
            pltpu.VMEM((ITERS, modes, cols), BF16),
            pltpu.VMEM((ITERS, 4, modes, cols), BF16),
            dma((4,)),
            dma((ITERS, 4)),
            dma((ITERS, 4)),
            dma((4,)),
            dma((4,)),
            dma((ITERS, 4)),
            dma((ITERS, 4)),
            dma((ITERS, nx)),
            dma((ITERS, nx)),
            dma((ITERS, ny)),
            dma((ITERS, ny)),
            dma((ITERS, 4)),
            dma((ITERS, 4)),
        ],
        compiler_params=pltpu.CompilerParams(
            collective_id=0, has_side_effects=True, vmem_limit_bytes=58 * 2**20
        ),
    )(dual_ops[0, 0], loads[0, 0], kernel_basis[0, 0], coarse_inverse[0, 0])
    return result[None, None]


def solution(mesh):
    placed = P("sx", "sy", None, None)
    return jax.shard_map(
        functools.partial(local, mesh.shape["sx"], mesh.shape["sy"]),
        mesh=mesh,
        in_specs=(placed,) * 4,
        out_specs=placed,
        check_vma=False,
    )
```

time: 76.2 us -> 65.4 us (0.86)
  Pallas kernels: 68.4 us -> 63 us
  local copies, waits for them, and re-layouts: 7.48 us -> 2.26 us
    pallas_call x1, Pallas kernels: 68.4 us -> 63 us  [local(): pl.pallas_call(functools.partial(iterate, nx, ny), out_shape=jax.ShapeDty...]
    unnamed x9 -> x1, local copies, waits for them, and re-layouts: 7.48 us -> 2.26 us
where the time goes in v2:
time: 65.4 us; the launch traced here: 65.3 us
  Pallas kernels  63 us (96%)
  local copies, waits for them, and re-layouts  2.26 us (3%)
    pallas_call x1, Pallas kernels, local(): pl.pallas_call(functools.partial(iterate, nx, ny), out_shape=jax.ShapeDty...  63 us
    unnamed x1, local copies, waits for them, and re-layouts  2.26 us

profile of v2, /device:TPU:0, one launch (start us, length us, event | category | flops | bytes accessed | tf_op | source)
XLA Modules:
  0.0 65.3 jit_solution(7625548607358634881)
XLA Ops:
  0.0 63.0 %shard_map.46 = f32[2048,128]{1,0:T(8,128)} custom-call(bf16[2048,2048]{1,0:T(8,128)(2,1)} %bitcast.5, f32[2048,128]{1,0:T(8,128)} %bitcast.7, bf16[64,2048]{1,0:T(8,128)(2,1)} %bitcast.8, bf16[256,512]{1,0:T(8,128)(2,1)} %bitcast.9), custom_call_target="tpu_custom_call" | custom-call | tf_op jit(solution)/shard_map/pallas_call | solution.py:344
  63.0 2.3 %copy.6 = f32[1,1,2048,128]{3,2,1,0:T(8,128)} copy(f32[1,1,2048,128]{3,2,1,0:T(8,128)} %bitcast.6) | data formatting | bytes 2097152

commit v3 on v2

--- a/solution.py
+++ b/solution.py
@@ -33,6 +33,7 @@
     spread_rows,
     image,
     gram,
+    gram_near,
     half,
     resid,
     base,
@@ -57,6 +58,8 @@
     slice_recv,
     near_send,
     near_recv,
+    gram_send,
+    gram_recv,
 ):
     a, b = lax.axis_index("sx"), lax.axis_index("sy")
     n, cols = loads.shape
@@ -65,6 +68,16 @@
     peers = ((a - 1, b), (a + 1, b), (a, b - 1), (a, b + 1))
     present = (a > 0, a < nx - 1, b > 0, b < ny - 1)
     opposite = (1, 0, 3, 2)
+    compass = ((-1, 0), (1, 0), (0, -1), (0, 1))
+    diagonal = ((-1, -1), (-1, 1), (1, -1), (1, 1))
+    straight = ((-2, 0), (2, 0), (0, -2), (0, 2))
+
+    def inside(offset):
+        row, column = a + offset[0], b + offset[1]
+        return (row >= 0) & (row < nx) & (column >= 0) & (column < ny)
+
+    def around(step):
+        return compass if step == ITERS - 1 else compass + diagonal + straight
 
     loads_copy = pltpu.make_async_copy(loads_hbm, loads, local_sem.at[0])
     basis_load = pltpu.make_async_copy(basis_hbm, basis, local_sem.at[1])
@@ -85,25 +98,45 @@
             barrier, inc=1, device_id=(a, lax.rem(b + k, ny)), device_id_type=MESH
         )
 
+    greeted = jnp.int32(nx - 1 + ny - 1)
+    for offset in diagonal:
+        greeted += inside(offset).astype(jnp.int32)
+
+        @pl.when(inside(offset))
+        def _():
+            pl.semaphore_signal(
+                barrier,
+                inc=1,
+                device_id=(a + offset[0], b + offset[1]),
+                device_id_type=MESH,
+            )
+
     def rows(f):
         return pl.ds(f * width, width)
 
+    for offset in compass + diagonal + straight:
+
+        @pl.when(jnp.logical_not(inside(offset)))
+        def _():
+            for step in range(ITERS):
+                coarse_near[step, 2 + offset[0], 2 + offset[1]] = jnp.zeros((modes, cols), BF16)
+
     for f in range(4):
 
         @pl.when(jnp.logical_not(present[f]))
         def _():
             for step in range(ITERS):
                 halo[step, f] = jnp.zeros(halo.shape[2:], BF16)
-                coarse_near[step, f] = jnp.zeros(coarse_near.shape[2:], BF16)
                 offers[step, f] = jnp.zeros(offers.shape[2:], BF16)
             beside_basis[f] = jnp.zeros(beside_basis.shape[1:], BF16)
+            gram_near[f] = jnp.zeros(gram_near.shape[1:], BF16)
 
     loads_copy.wait()
     for f in range(4):
         faces[0, f] = loads[rows(f), :].astype(BF16)
     basis_load.wait()
 
-    pl.semaphore_wait(barrier, nx - 1 + ny - 1)
+    pl.semaphore_wait(barrier, greeted)
 
     def to_face(src, dst, sends, recvs, f, slot):
         return pltpu.make_async_remote_copy(
@@ -145,15 +178,33 @@
             slot,
         )
 
-    def near_copy(step, f, slot):
+    def gram_copy(step, f, slot):
         return to_face(
-            coarse.at[step],
-            coarse_near.at[step, slot],
-            near_send.at[step, f],
-            near_recv.at[step, slot],
+            gram.at[pl.ds((f + 1) * modes, modes)],
+            gram_near.at[slot],
+            gram_send.at[f],
+            gram_recv.at[slot],
             f,
             slot,
         )
+
+    def near_copy(step, offset, sign):
+        place = (2 + sign * offset[0], 2 + sign * offset[1])
+        return pltpu.make_async_remote_copy(
+            src_ref=coarse.at[step],
+            dst_ref=coarse_near.at[step, *place],
+            send_sem=near_send.at[step, *place],
+            recv_sem=near_recv.at[step, *place],
+            device_id=(a + offset[0], b + offset[1]),
+            device_id_type=MESH,
+        )
+
+    def near_each(step, sign, what):
+        for offset in around(step):
+
+            @pl.when(inside(offset))
+            def _():
+                getattr(near_copy(step, offset, sign), what)()
 
     def gather_copy(step, k):
         return pltpu.make_async_remote_copy(
@@ -195,7 +246,19 @@
         return jnp.dot(x, y, preferred_element_type=F32)
 
     def with_near(step):
-        return jnp.concatenate([coarse[step]] + [coarse_near[step, f] for f in range(4)], axis=0)
+        return [block(step, at) for at in ((0, 0), *compass)]
+
+    def block(step, at):
+        if at == (0, 0):
+            return coarse[step]
+        return coarse_near[step, 2 + at[0], 2 + at[1]]
+
+    def with_far(step):
+        blocks = []
+        for centre in compass:
+            for at in ((0, 0), *compass):
+                blocks.append(block(step, (centre[0] + at[0], centre[1] + at[1])))
+        return jnp.concatenate(blocks, axis=0)
 
     def share(step, total):
         gathered[step, a] = total.astype(BF16)
@@ -216,8 +279,7 @@
             slice_copy(step, k).wait_recv()
             total += arrived[step, k].astype(F32)
         coarse[step] = total.astype(BF16)
-        for f in range(4):
-            send(near_copy, step, f)
+        near_each(step, -1, "start")
 
     def apply_dual(first, count):
         span = width // 2
@@ -229,16 +291,17 @@
                 dual[pl.ds(start, span), :], half[...]
             )
 
-    def to_modes(read):
+    def to_modes(step):
         own = jnp.zeros((modes, cols), F32)
         for f in range(4):
-            both = dot(spread_rows[f], read(f).astype(BF16))
+            both = dot(spread_rows[f], base[rows(f), :].astype(BF16))
             own += both[:modes]
-            base_modes[pl.ds((f + 1) * modes, modes), :] = both[modes:]
-        base_modes[pl.ds(0, modes), :] = own
+            offered[step, f] = both[modes:].astype(BF16)
+            send(offer_copy, step, f)
+        base_modes[...] = own
 
     def correct(step, f):
-        stacked = jnp.concatenate([coarse[step], coarse_near[step, f]], axis=0)
+        stacked = jnp.concatenate([coarse[step], block(step, compass[f])], axis=0)
         return DAMPING * dot(spread[rows(f), :], stacked)
 
     for f in range(4):
@@ -281,27 +344,29 @@
         own += both[:modes]
         gram[pl.ds((f + 1) * modes, modes), :] = both[modes:].astype(BF16)
     gram[pl.ds(0, modes), :] = own.astype(BF16)
+    for f in range(4):
+        send(gram_copy, 0, f)
     apply_dual(0, 8)
-    to_modes(lambda f: base[rows(f), :])
+    to_modes(0)
 
     for step in range(1, ITERS):
-        for f in range(4):
-            expect(near_copy, step - 1, f)
-        stack = with_near(step - 1)
-        total_modes = base_modes[...] + DAMPING * dot(gram[...], stack)
-        for f in range(4):
-            offered[step, f] = total_modes[(f + 1) * modes : (f + 2) * modes].astype(BF16)
-            send(offer_copy, step, f)
+        total = base_modes[...]
+        for f in range(4):
+            expect(offer_copy, step - 1, f)
+            total += offers[step - 1, f].astype(F32)
+            if step == 1:
+                expect(gram_copy, 0, f)
+        near_each(step - 1, 1, "wait_recv")
+        stack = jnp.concatenate(with_near(step - 1), axis=0)
+        change = dot(gram[pl.ds(0, modes), :], stack)
+        beside = jnp.concatenate([gram_near[f] for f in range(4)], axis=1)
+        change += dot(beside, with_far(step - 1))
+        share(step, total + DAMPING * change)
         for f in range(4):
             value = base[rows(f), :] + DAMPING * dot(image[rows(f), :], stack)
             resid[rows(f), :] = value
             faces[step, f] = value.astype(BF16)
             send(face_copy, step, f)
-        total = total_modes[:modes]
-        for f in range(4):
-            expect(offer_copy, step, f)
-            total += offers[step, f].astype(F32)
-        share(step, total)
         for f in range(4):
             out[rows(f), :] = out[rows(f), :] - correct(step - 1, f)
         spread_tiles(step)
@@ -316,20 +381,21 @@
         finish_coarse(step)
         if step < ITERS - 1:
             apply_dual(4, 4)
-            to_modes(lambda f: base[rows(f), :])
-
-    for f in range(4):
-        expect(near_copy, ITERS - 1, f)
+            to_modes(step)
+
+    near_each(ITERS - 1, 1, "wait_recv")
+    for f in range(4):
         out[rows(f), :] = out[rows(f), :] - correct(ITERS - 1, f)
 
     for f in range(4):
         sent(basis_copy, 0, f)
         for step in range(ITERS):
             sent(face_copy, step, f)
-            sent(near_copy, step, f)
-            if step:
+            if step < ITERS - 1:
                 sent(offer_copy, step, f)
+        sent(gram_copy, 0, f)
     for step in range(ITERS):
+        near_each(step, -1, "wait_send")
         for k in range(1, nx):
             gather_copy(step, k).wait_send()
         for k in range(1, ny):
@@ -358,17 +424,18 @@
             pltpu.VMEM((4, 2 * modes, width), BF16),
             pltpu.VMEM((n, 5 * modes), BF16),
             pltpu.VMEM((5 * modes, 5 * modes), BF16),
+            pltpu.VMEM((4, modes, 5 * modes), BF16),
             pltpu.VMEM((n, cols), BF16),
             pltpu.VMEM((n, cols), F32),
             pltpu.VMEM((n, cols), F32),
-            pltpu.VMEM((5 * modes, cols), F32),
+            pltpu.VMEM((modes, cols), F32),
             pltpu.VMEM((ITERS, 4, modes, cols), BF16),
             pltpu.VMEM((ITERS, 4, modes, cols), BF16),
             pltpu.VMEM((ITERS, nx, modes, cols), BF16),
             pltpu.VMEM((ITERS, ny, modes, cols), BF16),
             pltpu.VMEM((ITERS, ny, modes, cols), BF16),
             pltpu.VMEM((ITERS, modes, cols), BF16),
-            pltpu.VMEM((ITERS, 4, modes, cols), BF16),
+            pltpu.VMEM((ITERS, 5, 5, modes, cols), BF16),
             dma((4,)),
             dma((ITERS, 4)),
             dma((ITERS, 4)),
@@ -380,8 +447,10 @@
             dma((ITERS, nx)),
             dma((ITERS, ny)),
             dma((ITERS, ny)),
-            dma((ITERS, 4)),
-            dma((ITERS, 4)),
+            dma((ITERS, 5, 5)),
+            dma((ITERS, 5, 5)),
+            dma((4,)),
+            dma((4,)),
         ],
         compiler_params=pltpu.CompilerParams(
             collective_id=0, has_side_effects=True, vmem_limit_bytes=58 * 2**20

time: 65.4 us -> 64.3 us (0.983)
  Pallas kernels: 63 us -> 61.9 us
    pallas_call x1, Pallas kernels: 63 us -> 61.9 us  [local(): pl.pallas_call(functools.partial(iterate, nx, ny), out_shape=jax.ShapeDty...]
where the time goes in v3:
time: 64.3 us; the launch traced here: 64.1 us
  Pallas kernels  61.9 us (96%)
  local copies, waits for them, and re-layouts  2.26 us (4%)
    pallas_call x1, Pallas kernels, local(): pl.pallas_call(functools.partial(iterate, nx, ny), out_shape=jax.ShapeDty...  61.9 us
    unnamed x1, local copies, waits for them, and re-layouts  2.26 us

profile of v3, /device:TPU:0, one launch (start us, length us, event | category | flops | bytes accessed | tf_op | source)
XLA Modules:
  0.0 64.1 jit_solution(3964978393253338045)
XLA Ops:
  0.0 61.9 %shard_map.46 = f32[2048,128]{1,0:T(8,128)} custom-call(bf16[2048,2048]{1,0:T(8,128)(2,1)} %bitcast.5, f32[2048,128]{1,0:T(8,128)} %bitcast.7, bf16[64,2048]{1,0:T(8,128)(2,1)} %bitcast.8, bf16[256,512]{1,0:T(8,128)(2,1)} %bitcast.9), custom_call_target="tpu_custom_call" | custom-call | tf_op jit(solution)/shard_map/pallas_call | solution.py:410
  61.9 2.3 %copy.6 = f32[1,1,2048,128]{3,2,1,0:T(8,128)} copy(f32[1,1,2048,128]{3,2,1,0:T(8,128)} %bitcast.6) | data formatting | bytes 2097152
